TPU v7x, 32 devices: a whole 2x2x4 slice. The times are simulated.
32 devices in a mesh: file: 16 (over z, y, core), win: 2 (over x).
Axes of the slice: x: 2, y: 2, z: 4, core: 2. Of those that a mesh axis runs over, the one named last changes fastest.
Arguments:
- raw: bfloat16 [2, 128, 20480], P('win', None, 'file'), may hold values from -60 to 60
- fir_taps: float32 [64], replicated, may hold values from -0.75 to 0.75
- offsets: int32 [2, 16], P('win', 'file'), may hold values from 0 to 9
- vs_index: int32 [64], replicated, may hold values from 0 to 127, as said below
Outputs:
- correlation: float32 [64, 128, 2048], P('win', 'file')
Inputs may be any that keep to these rules, and one draw needn't show every extreme that they name: `vs_index`: virtual source s is one of the channels s * 2 to s * 2 + 1.
All inputs are finite; a program needn't handle non-finite values.
Results may differ from a plain program's by a relative error of at most 0.0063.
Values may be sent and summed in bfloat16 or wider, within the bound.
No kernel may reach another device: no remote copies, remote signals or barrier semaphores. Data moves between devices by JAX's collectives and lax.ppermute only.
A program may use at most 128 MiB of HBM per device.

v0:
```python
import math
import jax
import jax.numpy as jnp
from jax import lax
from jax.sharding import PartitionSpec as P

R = 10
TAPS = 64
TD = 128
SEG = 2048
BAND = 64
VS_DEV = 4
PRECISE = lax.Precision.HIGHEST
EPSILON = 1e-06


def phase_table(height, breadth, period_len):
    row_index = lax.broadcasted_iota(jnp.int32, (height, breadth), 0)
    col_index = lax.broadcasted_iota(jnp.int32, (height, breadth), 1)
    residue = row_index * col_index % period_len
    angles = residue.astype(jnp.float32) * (2.0 * math.pi / period_len)
    return (jnp.cos(angles), jnp.sin(angles))


def forward_spectrum(samples):
    length = samples.shape[-1]
    factor = min(128, length)
    inner = length // factor
    outer = 2 * length // factor
    half_factor = factor // 2
    leading = samples.shape[:-1]
    arranged = samples.astype(jnp.float32).reshape(leading + (inner, factor))
    cos_a, sin_a = phase_table(inner, outer, outer)
    first_re = jnp.einsum("...pa,pm->...ma", arranged, cos_a, precision=PRECISE)
    first_im = -jnp.einsum("...pa,pm->...ma", arranged, sin_a, precision=PRECISE)
    cos_t, sin_t = phase_table(outer, factor, 2 * length)
    twist_re = first_re * cos_t + first_im * sin_t
    twist_im = first_im * cos_t - first_re * sin_t
    cos_b, sin_b = phase_table(factor, half_factor, factor)
    out_re = jnp.einsum("...ma,an->...nm", twist_re, cos_b, precision=PRECISE) + jnp.einsum(
        "...ma,an->...nm", twist_im, sin_b, precision=PRECISE
    )
    out_im = jnp.einsum("...ma,an->...nm", twist_im, cos_b, precision=PRECISE) - jnp.einsum(
        "...ma,an->...nm", twist_re, sin_b, precision=PRECISE
    )
    return (out_re.reshape(leading + (length,)), out_im.reshape(leading + (length,)))


def inverse_lags(cross_re, cross_im):
    length = cross_re.shape[-1]
    factor = min(128, length)
    inner = length // factor
    outer = 2 * length // factor
    half_factor = factor // 2
    leading = cross_re.shape[:-1]
    quarter = jnp.arange(length, dtype=jnp.int32) % 4
    rotate_c = jnp.where(quarter == 0, 1.0, jnp.where(quarter == 2, -1.0, 0.0)).astype(jnp.float32)
    rotate_s = jnp.where(quarter == 1, 1.0, jnp.where(quarter == 3, -1.0, 0.0)).astype(jnp.float32)
    turned_re = (cross_re * rotate_c + cross_im * rotate_s).reshape(leading + (inner, factor))
    turned_im = (cross_im * rotate_c - cross_re * rotate_s).reshape(leading + (inner, factor))
    cos_a, sin_a = phase_table(inner, outer, outer)
    first_re = jnp.einsum("...pa,pm->...ma", turned_re, cos_a, precision=PRECISE) - jnp.einsum(
        "...pa,pm->...ma", turned_im, sin_a, precision=PRECISE
    )
    first_im = jnp.einsum("...pa,pm->...ma", turned_re, sin_a, precision=PRECISE) + jnp.einsum(
        "...pa,pm->...ma", turned_im, cos_a, precision=PRECISE
    )
    cos_t, sin_t = phase_table(outer, factor, 2 * length)
    twist_re = first_re * cos_t - first_im * sin_t
    twist_im = first_re * sin_t + first_im * cos_t
    cos_b, sin_b = phase_table(factor, half_factor, factor)
    lagged = jnp.einsum("...ma,an->...nm", twist_re, cos_b, precision=PRECISE) - jnp.einsum(
        "...ma,an->...nm", twist_im, sin_b, precision=PRECISE
    )
    return lagged.reshape(leading + (length,))


def whiten(spec_re, spec_im):
    length = spec_re.shape[-1]
    leading = spec_re.shape[:-1]
    magnitude = jnp.sqrt(spec_re * spec_re + spec_im * spec_im)
    amplitude = (
        jnp.mean(magnitude.reshape(leading + (length // BAND, BAND)), axis=-1, keepdims=True)
        + EPSILON
    )
    white_re = (spec_re.reshape(leading + (length // BAND, BAND)) / amplitude).reshape(
        leading + (length,)
    )
    white_im = (spec_im.reshape(leading + (length // BAND, BAND)) / amplitude).reshape(
        leading + (length,)
    )
    return (white_re.astype(jnp.bfloat16), white_im.astype(jnp.bfloat16))


def band_matrix(fir_taps, block_width):
    span = R * block_width + TAPS - R
    period_len = span + R
    flipped = fir_taps[::-1].astype(jnp.bfloat16)
    pattern = jnp.concatenate([flipped, jnp.zeros((period_len - TAPS,), jnp.bfloat16)])
    flat = jnp.tile(pattern, block_width)[: block_width * span]
    return flat.reshape(block_width, span).T


def decimate(extended, offset_now, band_taps):
    row_count = extended.shape[0]
    block_width = band_taps.shape[1]
    span = R * (TD - 1) + TAPS
    segment = lax.dynamic_slice_in_dim(extended, offset_now + 1, span, axis=1)
    block_count = TD // block_width
    stride_len = R * block_width
    leading_part = segment[:, : stride_len * block_count].reshape(
        row_count, block_count, stride_len
    )
    trailing = segment[:, stride_len:]
    trailing = jnp.pad(trailing, ((0, 0), (0, stride_len * block_count - trailing.shape[1])))
    trailing = trailing.reshape(row_count, block_count, stride_len)[:, :, : TAPS - R]
    blocks = jnp.concatenate([leading_part, trailing], axis=2)
    result = jnp.einsum("cbi,io->cbo", blocks, band_taps, preferred_element_type=jnp.float32)
    return result.reshape(row_count, TD)


def local(raw, fir_taps, offsets, vs_index):
    samples = raw[0]
    file_count = lax.axis_size("file")
    win_count = lax.axis_size("win")
    band_taps = band_matrix(fir_taps, math.gcd(TD, 128))
    regrouped = lax.all_to_all(samples, "file", split_axis=0, concat_axis=1, tiled=True)
    shifts = lax.all_gather(offsets, "file", axis=1, tiled=True)
    row_count = regrouped.shape[0]
    file_blocks = regrouped.reshape(row_count, file_count, regrouped.shape[1] // file_count)
    previous = jnp.concatenate(
        [
            jnp.zeros((row_count, 1, TAPS), file_blocks.dtype),
            file_blocks[:, :-1, file_blocks.shape[2] - TAPS :],
        ],
        axis=1,
    )
    extended = jnp.concatenate([previous, file_blocks], axis=2)
    pieces = jax.vmap(decimate, in_axes=(1, 0, None), out_axes=1)(extended, shifts[0], band_taps)
    owned = pieces.reshape(row_count, file_count * TD).astype(jnp.bfloat16)
    row_count = owned.shape[0]
    seg_count = owned.shape[1] // SEG
    own_re, own_im = forward_spectrum(owned.reshape(row_count, seg_count, SEG))
    white_re, white_im = whiten(own_re, own_im)
    file_pos = lax.axis_index("file")
    source_rows = (
        lax.dynamic_slice_in_dim(vs_index, file_pos * VS_DEV, VS_DEV) - file_pos * row_count
    )
    source_re, source_im = (
        lax.all_gather(jnp.take(white_re, source_rows, axis=0), "file", axis=0, tiled=True),
        lax.all_gather(jnp.take(white_im, source_rows, axis=0), "file", axis=0, tiled=True),
    )
    own_both = jnp.concatenate([white_re, white_im], axis=1)
    scale_out = 1.0 / math.sqrt(SEG * seg_count * win_count)
    paired = jnp.stack(
        [
            jnp.concatenate([source_re, source_im], axis=1),
            jnp.concatenate([-source_im, source_re], axis=1),
        ],
        axis=1,
    )
    joined = jnp.einsum("cqf,sdqf->scdf", own_both, paired, preferred_element_type=jnp.float32)
    stacked = lax.psum_scatter(
        joined.reshape(joined.shape[0], joined.shape[1], 2 * SEG),
        "win",
        scatter_dimension=0,
        tiled=True,
    )
    return inverse_lags(stacked[..., :SEG], stacked[..., SEG:]) * scale_out


def solution(mesh):
    return jax.shard_map(
        local,
        mesh=mesh,
        in_specs=(P("win", None, "file"), P(), P("win", "file"), P()),
        out_specs=P("win", "file", None),
        check_vma=False,
    )
```

profile of v0, /device:TPU:0, one launch (start us, length us, event | category | flops | bytes accessed | tf_op | source)
XLA Modules:
  0.0 293.7 jit_solution(40036436673634234)
XLA Ops:
  6.5 7.4 %all-to-all-start = ((bf16[16,8,1280]{2,1,0:T(8,128)(2,1)}), bf16[16,8,1280]{2,1,0:T(8,128)(2,1)S(1)}, u32[]{:S(2)}, u32[]{:S(2)}) async-start(bf16[16,8,1280]{2,1,0:T(8,128)(2,1)} %bitcast.144), calls=%async_computation | async-start | bytes 655360 | tf_op jit(solution)/shard_map/all_to_all | solution.py:127
  14.6 1.3 dynamic-slice.4
  15.9 0.6 bitcast_dynamic-update-slice_fusion
  16.5 0.7 compare_and_fusion
  17.3 12.4 %all-reduce.4 = s32[16]{0:T(128)S(1)} all-reduce(s32[16]{0:T(128)S(1)} %bitcast_dynamic-update-slice_fusion), channel_id=1, replica_groups=mesh['file'=16,'win'=2] {'file'}, use_global_device_ids=true, to_apply=%add.4 | all-reduce | flops 16 | bytes 128
  29.7 0.7 rev.3
  30.8 0.7 reshape.232
  31.9 29.9 %while.1 = (s32[]{:T(128)}, bf16[16,8,1344]{2,1,0:T(8,128)(2,1)S(1)}, s32[16,3]{0,1:T(4,128)S(1)}, bf16[16,8,1334]{2,1,0:T(8,128)(2,1)S(1)}, s32[]{:T(128)}) while((s32[]{:T(128)}, bf16[16,8,1344]{2,1,0:T(8,128)(2,1)S(1)}, s32[16,3]{0,1:T(4,128)S(1)}, bf16[16,8,1334]{2,1,0:T(8,128)(2,1)S(1)}, s32[]{:T(128)}) %tuple.29), condition=%wide.while_cond, body=%wide.while_body.sunk | while | flops 2 | bytes 45173 | solution.py:108
  32.0 0.5 fusion.149
  32.5 1.3 dynamic-slice_dynamic-update-slice_fusion.2
  33.9 0.5 fusion.149
  34.4 1.3 dynamic-slice_dynamic-update-slice_fusion.2
  35.7 0.5 fusion.149
  36.3 1.3 dynamic-slice_dynamic-update-slice_fusion.2
  37.6 0.5 fusion.149
  38.1 1.3 dynamic-slice_dynamic-update-slice_fusion.2
  39.5 0.5 fusion.149
  40.0 1.3 dynamic-slice_dynamic-update-slice_fusion.2
  41.3 0.5 fusion.149
  41.9 1.3 dynamic-slice_dynamic-update-slice_fusion.2
  43.2 0.5 fusion.149
  43.7 1.3 dynamic-slice_dynamic-update-slice_fusion.2
  45.1 0.5 fusion.149
  45.6 1.3 dynamic-slice_dynamic-update-slice_fusion.2
  47.0 0.5 fusion.149
  47.5 1.3 dynamic-slice_dynamic-update-slice_fusion.2
  48.8 0.5 fusion.149
  49.4 1.3 dynamic-slice_dynamic-update-slice_fusion.2
  50.7 0.5 fusion.149
  51.2 1.3 dynamic-slice_dynamic-update-slice_fusion.2
  52.6 0.5 fusion.149
  53.1 1.3 dynamic-slice_dynamic-update-slice_fusion.2
  54.4 0.5 fusion.149
  55.0 1.3 dynamic-slice_dynamic-update-slice_fusion.2
  56.3 0.5 fusion.149
  56.8 1.3 dynamic-slice_dynamic-update-slice_fusion.2
  58.2 0.5 fusion.149
  58.7 1.3 dynamic-slice_dynamic-update-slice_fusion.2
  60.0 0.5 fusion.149
  60.6 1.3 dynamic-slice_dynamic-update-slice_fusion.2
  62.8 0.4 fusion.33
  63.2 0.4 fusion.35
  63.6 0.4 fusion.23
  64.2 0.5 sqrt_reduce_fusion
  65.5 0.7 copy.91
  66.3 0.6 gather_fusion
  66.8 0.6 gather_fusion.1
  67.5 19.4 %all_gather.11 = bf16[64,1,2048]{2,1,0:T(2,128)(2,1)S(1)} all-gather(bf16[4,1,2048]{2,1,0:T(2,128)(2,1)S(1)} %copy.77), channel_id=1, replica_groups=mesh['file'=16,'win'=2] {'file'}, dimensions={0}, use_global_device_ids=true | all-gather | bytes 278528 | tf_op jit(solution)/shard_map/all_gather | solution.py:151
  87.1 19.7 %all_gather.10 = bf16[64,1,2048]{2,1,0:T(2,128)(2,1)S(1)} all-gather(bf16[4,1,2048]{2,1,0:T(2,128)(2,1)S(1)} %copy.75), channel_id=1, replica_groups=mesh['file'=16,'win'=2] {'file'}, dimensions={0}, use_global_device_ids=true | all-gather | bytes 278528 | tf_op jit(solution)/shard_map/all_gather | solution.py:150
  107.1 1.1 pad_maximum_fusion
  108.2 4.5 %copy.82 = bf16[64,2,2,2048]{0,2,1,3:T(2,128)(2,1)S(1)} copy(bf16[64,2,2,2048]{3,0,2,1:T(8,128)(2,1)} %pad_maximum_fusion) | data formatting | bytes 2097152 | tf_op jit(solution)/shard_map/stack | solution.py:155
  112.7 6.9 %convolution_bitcast_fusion = f32[64,8,2,2048]{0,1,2,3:T(8,128)} fusion(bf16[64,2,2,2048]{0,2,1,3:T(2,128)(2,1)S(1)} %copy.82, bf16[8,2,2048,1]{0,1,3,2:T(2,128)(2,1)S(1)} %copy.91), kind=kOutput, calls=%fused_computation.4 | convolution fusion | flops 8388608 | bytes 9502720 | tf_op jit(solution)/shard_map/cqf,sdqf->scdf/dot_general | solution.py:162
  119.6 17.3 %copy.84 = f32[64,8,2,2048]{3,2,1,0:T(2,128)} copy(f32[64,8,2,2048]{0,1,2,3:T(8,128)} %convolution_bitcast_fusion) | data formatting | bytes 16777216 | tf_op jit(solution)/shard_map/cqf,sdqf->scdf/transpose | solution.py:162
  136.8 11.8 %reshape.235 = f32[64,8,4096]{2,1,0:T(8,128)} reshape(f32[64,8,2,2048]{3,2,1,0:T(2,128)} %copy.84) | data formatting | bytes 16777216 | tf_op jit(solution)/shard_map/reshape | solution.py:164
  148.7 97.1 %reduce-scatter.2.cloned.1.call-done = f32[32,8,4096]{2,1,0:T(8,128)} async-done(((f32[64,8,4096]{2,1,0:T(8,128)}), f32[32,8,4096]{2,1,0:T(8,128)}) %reduce-scatter.2.cloned.1.call-update) | async-done | bytes 4194320 | tf_op jit(solution)/shard_map/reduce_scatter | solution.py:163
  245.8 2.8 subtract_bitcast_fusion
  248.6 3.5 %fusion.20 = f32[32,32,8,128]{3,0,2,1:T(8,128)S(1)} fusion(f32[32,8,16,128]{3,1,2,0:T(8,128)S(1)} %get-tuple-element.29), kind=kOutput, calls=%fused_computation.28 | convolution fusion | flops 201333760 | bytes 6291456 | tf_op jit(solution)/shard_map/...pa,pm->...ma/dot_general | solution.py:62
  252.1 3.7 %fusion.18 = f32[32,32,8,128]{3,0,2,1:T(8,128)S(1)} fusion(f32[32,8,16,128]{3,1,2,0:T(8,128)S(1)} %get-tuple-element.29), kind=kOutput, calls=%fused_computation.26 | convolution fusion | flops 201333760 | bytes 6291456 | tf_op jit(solution)/shard_map/...pa,pm->...ma/dot_general | solution.py:65
  255.8 3.6 %convolution_subtract_fusion = f32[32,32,8,128]{3,0,2,1:T(8,128)S(1)} fusion(f32[32,32,8,128]{3,0,2,1:T(8,128)S(1)} %fusion.20, f32[32,8,16,128]{3,1,2,0:T(8,128)S(1)} %get-tuple-element.28), kind=kOutput, calls=%fused_computation.17 | convolution fusion | flops 202382336 | bytes 10485760 | tf_op jit(solution)/shard_map/...pa,pm->...ma/dot_general | solution.py:62
  259.4 4.2 %convolution_add_fusion = f32[32,32,8,128]{3,0,2,1:T(8,128)S(1)} fusion(f32[32,32,8,128]{3,0,2,1:T(8,128)S(1)} %fusion.18, f32[32,8,16,128]{3,1,2,0:T(8,128)S(1)} %get-tuple-element.28), kind=kOutput, calls=%fused_computation.16 | convolution fusion | flops 202382336 | bytes 10485760 | tf_op jit(solution)/shard_map/...pa,pm->...ma/dot_general | solution.py:65
  263.6 3.5 %fusion = f32[64,32,8,32]{0,3,2,1:T(8,128)S(1)} fusion(f32[32,32,8,128]{3,0,2,1:T(8,128)S(1)} %convolution_add_fusion, f32[32,32,8,128]{3,0,2,1:T(8,128)S(1)} %convolution_subtract_fusion, f32[32,128]{1,0:T(8,128)S(1)} %get-tuple-element.38, f32[32,128]{1,0:T(8,128)S(1)} %get-tuple-element.39), kind=kOutput, calls=%fused_computation.5 | convolution fusion | flops 808566784 | bytes 10518528 | tf_op jit(solution)/shard_map/...ma,an->...nm/dot_general | solution.py:72
  267.1 5.3 %multiply_bitcast_fusion = f32[32,8,64,32]{2,3,1,0:T(8,128)} fusion(f32[64,32,8,32]{0,3,2,1:T(8,128)S(1)} %fusion, f32[32,32,8,128]{3,0,2,1:T(8,128)S(1)} %convolution_add_fusion, f32[32,32,8,128]{3,0,2,1:T(8,128)S(1)} %convolution_subtract_fusion, f32[32,128]{1,0:T(8,128)S(1)} %get-tuple-element.38, f32[32,128]{1,0:T(8,128)S(1)} %get-tuple-element.39), kind=kOutput, calls=%fused_computation.9 | convolution fusion | flops 809615360 | bytes 12615680 | tf_op jit(solution)/shard_map/...ma,an->...nm/dot_general | solution.py:72
  272.4 6.9 %copy.89 = f32[32,8,64,32]{3,2,1,0:T(8,128)} copy(f32[32,8,64,32]{2,3,1,0:T(8,128)} %multiply_bitcast_fusion) | data formatting | bytes 4194304 | tf_op jit(solution)/shard_map/mul | solution.py:169
  279.3 7.5 %mul.267 = f32[32,8,2048]{2,1,0:T(8,128)} reshape(f32[32,8,64,32]{3,2,1,0:T(8,128)} %copy.89) | data formatting | bytes 4194304 | tf_op jit(solution)/shard_map/mul | solution.py:169
  (58 shorter events, 4.4 us)
Async XLA Ops:
  6.5 25.1 %all-to-all-start = ((bf16[16,8,1280]{2,1,0:T(8,128)(2,1)}), bf16[16,8,1280]{2,1,0:T(8,128)(2,1)S(1)}, u32[]{:S(2)}, u32[]{:S(2)}) async-start(bf16[16,8,1280]{2,1,0:T(8,128)(2,1)} %bitcast.144), calls=%async_computation | async-start | bytes 655360 | tf_op jit(solution)/shard_map/all_to_all | solution.py:127
  13.9 231.8 %reduce-scatter.2.cloned.1.call-start = ((), (), s32[]{:S(2)}) async-start(), calls=%async_computation.2 | async-start | bytes 12582912 | tf_op jit(solution)/shard_map/reduce_scatter | solution.py:163
Sparse Core Ops, SparseCore 0:
  148.8 96.9 reduce-scatter.1
where the time goes:
time: 295 us; the launch traced here: 294 us
  waiting for transfers between devices  97.1 us (33%)
  local copies, waits for them, and re-layouts  84.7 us (29%)
  blocking collectives  51.5 us (17%)
  matrix products  33.2 us (11%)
  between operations  14.4 us (5%)
  starting transfers between devices  7.43 us (3%)
  other arithmetic  5.31 us (2%)
    reduce_scatter x1, waiting for transfers between devices, local(): lax.psum_scatter(joined.reshape(joined.shape[0], joined.shape[1], 2 * SEG...  97.1 us
    gather x48, local copies, waits for them, and re-layouts  29.9 us
    all_gather x1, blocking collectives, local(): lax.all_gather(jnp.take(white_re, source_rows, axis=0), 'file', axis=0, t...  19.7 us
    all_gather x1, blocking collectives, local(): lax.all_gather(jnp.take(white_im, source_rows, axis=0), 'file', axis=0, t...  19.4 us
    transpose x1, local copies, waits for them, and re-layouts, local(): jnp.einsum('cqf,sdqf->scdf', own_both, paired, preferred_element_type=jnp...  17.3 us
    mul x2, local copies, waits for them, and re-layouts, local(): return inverse_lags(stacked[..., :SEG], stacked[..., SEG:]) * scale_out  14.4 us
    unnamed x1, blocking collectives  12.4 us
    reshape x1, local copies, waits for them, and re-layouts, local(): joined.reshape(joined.shape[0], joined.shape[1], 2 * SEG)  11.8 us
  transfers between devices with their start and end apart: 2, of which 1 were waited for; matrix products, arithmetic and copies ran while one was open for 2% of the time, Pallas kernels for 0%

commit v1 on v0

--- a/solution.py
+++ b/solution.py
@@ -12,6 +12,17 @@
 VS_DEV = 4
 PRECISE = lax.Precision.HIGHEST
 EPSILON = 1e-06
+
+
+def feed_face(obj, pos_dim, local_values):
+    before, p_next = (obj.shape[:pos_dim], obj.shape[pos_dim + 1 :])
+    return jnp.moveaxis(obj.reshape(*before, local_values, -1, *p_next), pos_dim, 0)
+
+
+def edges_handle(page, axis_no):
+    y_new = list(page.shape[1:])
+    y_new[axis_no] *= page.shape[0]
+    return jnp.moveaxis(page, 0, axis_no).reshape(y_new)
 
 
 def phase_table(height, breadth, period_len):
@@ -124,7 +135,16 @@
     file_count = lax.axis_size("file")
     win_count = lax.axis_size("win")
     band_taps = band_matrix(fir_taps, math.gcd(TD, 128))
-    regrouped = lax.all_to_all(samples, "file", split_axis=0, concat_axis=1, tiled=True)
+    h_now, out_arr = (lax.psum(1, "file"), lax.axis_index("file"))
+    known = feed_face(samples, 0, h_now)
+    nodes = [known[out_arr]]
+    for p in tuple(range(1, h_now)):
+        back = known[(out_arr + p) % h_now]
+        nodes.append(
+            lax.ppermute(back, "file", [(dev_j, (dev_j + p) % h_now) for dev_j in range(h_now)])
+        )
+    known = jnp.stack(nodes, axis=0)[(out_arr - jnp.arange(h_now)) % h_now]
+    regrouped = edges_handle(known, 1)
     shifts = lax.all_gather(offsets, "file", axis=1, tiled=True)
     row_count = regrouped.shape[0]
     file_blocks = regrouped.reshape(row_count, file_count, regrouped.shape[1] // file_count)

time: 295 us -> 320 us (1.085)
  starting transfers between devices: 7.43 us -> 21.2 us
  local copies, waits for them, and re-layouts: 84.7 us -> 90.8 us
    ppermute x0 -> x15, starting transfers between devices: none -> 21.2 us  [local(): lax.ppermute(back, 'file', [(dev_j, (dev_j + p) % h_now) for dev_j in ran...]
    all_to_all x1 -> x0, starting transfers between devices: 7.39 us -> none  [local(): lax.all_to_all(samples, 'file', split_axis=0, concat_axis=1, tiled=True)]
    gather x48 -> x49, local copies, waits for them, and re-layouts: 29.9 us -> 34.8 us
    all_gather x1, blocking collectives: 19.4 us -> 23 us  [local(): lax.all_gather(jnp.take(white_im, source_rows, axis=0), 'file', axis=0, t...]
  transfers between devices with their start and end apart: 2 -> 16, of which waited for: 1 -> 3; matrix products, arithmetic and copies ran while one was open for 2% -> 1% of each run, Pallas kernels for 0% -> 0%
where the time goes in v1:
time: 320 us; the launch traced here: 318 us
  waiting for transfers between devices  99.3 us (31%)
  local copies, waits for them, and re-layouts  90.8 us (28%)
  blocking collectives  54 us (17%)
  matrix products  33.2 us (10%)
  starting transfers between devices  21.2 us (7%)
  between operations  14.5 us (5%)
  other arithmetic  5.33 us (2%)
    reduce_scatter x1, waiting for transfers between devices, local(): lax.psum_scatter(joined.reshape(joined.shape[0], joined.shape[1], 2 * SEG...  97.8 us
    gather x48, local copies, waits for them, and re-layouts  34.2 us
    all_gather x1, blocking collectives, local(): lax.all_gather(jnp.take(white_im, source_rows, axis=0), 'file', axis=0, t...  23 us
    ppermute x15, starting transfers between devices, local(): lax.ppermute(back, 'file', [(dev_j, (dev_j + p) % h_now) for dev_j in ran...  21.2 us
    all_gather x1, blocking collectives, local(): lax.all_gather(jnp.take(white_re, source_rows, axis=0), 'file', axis=0, t...  18.9 us
    transpose x1, local copies, waits for them, and re-layouts, local(): jnp.einsum('cqf,sdqf->scdf', own_both, paired, preferred_element_type=jnp...  17.3 us
    mul x2, local copies, waits for them, and re-layouts, local(): return inverse_lags(stacked[..., :SEG], stacked[..., SEG:]) * scale_out  14.4 us
    unnamed x1, blocking collectives  12 us
  transfers between devices with their start and end apart: 16, of which 3 were waited for; matrix products, arithmetic and copies ran while one was open for 1% of the time, Pallas kernels for 0%

profile of v1, /device:TPU:0, one launch (start us, length us, event | category | flops | bytes accessed | tf_op | source)
XLA Modules:
  0.0 318.2 jit_solution(4495471105605138776)
XLA Ops:
  6.5 0.9 dynamic-slice_bitcast_fusion
  8.0 2.6 collective-permute-start.1
  10.6 2.4 collective-permute-start.2
  13.0 1.6 collective-permute-start.3
  15.5 1.3 dynamic-slice.4
  16.8 0.7 bitcast_dynamic-update-slice_fusion
  17.6 12.0 %all-reduce.4 = s32[16]{0:T(128)S(1)} all-reduce(s32[16]{0:T(128)S(1)} %bitcast_dynamic-update-slice_fusion), channel_id=1, replica_groups=mesh['file'=16,'win'=2] {'file'}, use_global_device_ids=true, to_apply=%add.4 | all-reduce | flops 16 | bytes 128
  29.6 0.7 compare_and_fusion
  30.4 0.7 rev.3
  31.5 0.7 reshape.275
  32.2 1.4 collective-permute-start.5
  34.2 2.3 collective-permute-start.8
  36.5 3.3 %collective-permute-start.9 = (bf16[8,1280]{1,0:T(8,128)(2,1)S(1)}, bf16[8,1280]{1,0:T(8,128)(2,1)S(1)}, u32[]{:S(2)}, u32[]{:S(2)}) collective-permute-start(bf16[8,1280]{1,0:T(8,128)(2,1)S(1)} %get-tuple-element.35), channel_id=1, source_target_pairs={{0,20},{2,22},{4,24},{6,26},{8,28},{10,30},{12,0},{14,2},{16,4},{1... | collective-permute-start | bytes 61448 | tf_op jit(solution)/shard_map/ppermute | solution.py:144
  39.8 0.6 collective-permute-start.10
  40.4 1.8 collective-permute-start.11
  42.7 2.3 collective-permute-start.13
  45.0 1.2 collective-permute-start.14
  46.5 1.2 collective-permute-done.14
  48.6 34.2 %while.1 = (s32[]{:T(128)}, bf16[16,8,1344]{2,1,0:T(8,128)(2,1)S(1)}, s32[16,3]{0,1:T(4,128)S(1)}, bf16[16,8,1334]{2,1,0:T(8,128)(2,1)S(1)}, s32[]{:T(128)}) while((s32[]{:T(128)}, bf16[16,8,1344]{2,1,0:T(8,128)(2,1)S(1)}, s32[16,3]{0,1:T(4,128)S(1)}, bf16[16,8,1334]{2,1,0:T(8,128)(2,1)S(1)}, s32[]{:T(128)}) %tuple.44), condition=%wide.while_cond, body=%wide.while_body.sunk | while | flops 2 | bytes 45173 | solution.py:119
  49.2 1.5 dynamic-slice_dynamic-update-slice_fusion.2
  50.8 0.6 fusion.151
  51.4 1.5 dynamic-slice_dynamic-update-slice_fusion.2
  52.9 0.6 fusion.151
  53.5 1.5 dynamic-slice_dynamic-update-slice_fusion.2
  55.1 0.6 fusion.151
  55.7 1.5 dynamic-slice_dynamic-update-slice_fusion.2
  57.8 1.5 dynamic-slice_dynamic-update-slice_fusion.2
  59.3 0.6 fusion.151
  59.9 1.5 dynamic-slice_dynamic-update-slice_fusion.2
  61.5 0.6 fusion.151
  62.1 1.5 dynamic-slice_dynamic-update-slice_fusion.2
  64.2 1.5 dynamic-slice_dynamic-update-slice_fusion.2
  65.7 0.6 fusion.151
  66.3 1.5 dynamic-slice_dynamic-update-slice_fusion.2
  67.9 0.6 fusion.151
  68.5 1.5 dynamic-slice_dynamic-update-slice_fusion.2
  70.0 0.6 fusion.151
  70.6 1.5 dynamic-slice_dynamic-update-slice_fusion.2
  72.8 1.5 dynamic-slice_dynamic-update-slice_fusion.2
  74.3 0.6 fusion.151
  74.9 1.5 dynamic-slice_dynamic-update-slice_fusion.2
  76.4 0.6 fusion.151
  77.0 1.5 dynamic-slice_dynamic-update-slice_fusion.2
  78.6 0.6 fusion.151
  79.2 1.5 dynamic-slice_dynamic-update-slice_fusion.2
  81.3 1.5 dynamic-slice_dynamic-update-slice_fusion.2
  86.5 0.7 copy.91
  88.5 23.0 %all_gather.11 = bf16[64,1,2048]{2,1,0:T(2,128)(2,1)S(1)} all-gather(bf16[4,1,2048]{2,1,0:T(2,128)(2,1)S(1)} %copy.77), channel_id=1, replica_groups=mesh['file'=16,'win'=2] {'file'}, dimensions={0}, use_global_device_ids=true | all-gather | bytes 278528 | tf_op jit(solution)/shard_map/all_gather | solution.py:171
  111.7 18.9 %all_gather.10 = bf16[64,1,2048]{2,1,0:T(2,128)(2,1)S(1)} all-gather(bf16[4,1,2048]{2,1,0:T(2,128)(2,1)S(1)} %copy.75), channel_id=1, replica_groups=mesh['file'=16,'win'=2] {'file'}, dimensions={0}, use_global_device_ids=true | all-gather | bytes 278528 | tf_op jit(solution)/shard_map/all_gather | solution.py:170
  130.9 1.1 pad_maximum_fusion
  131.9 4.5 %copy.82 = bf16[64,2,2,2048]{0,2,1,3:T(2,128)(2,1)S(1)} copy(bf16[64,2,2,2048]{3,0,2,1:T(8,128)(2,1)} %pad_maximum_fusion) | data formatting | bytes 2097152 | tf_op jit(solution)/shard_map/stack | solution.py:175
  136.5 6.9 %convolution_bitcast_fusion = f32[64,8,2,2048]{0,1,2,3:T(8,128)} fusion(bf16[64,2,2,2048]{0,2,1,3:T(2,128)(2,1)S(1)} %copy.82, bf16[8,2,2048,1]{0,1,3,2:T(2,128)(2,1)S(1)} %copy.91), kind=kOutput, calls=%fused_computation.5 | convolution fusion | flops 8388608 | bytes 9502720 | tf_op jit(solution)/shard_map/cqf,sdqf->scdf/dot_general | solution.py:182
  143.3 17.3 %copy.84 = f32[64,8,2,2048]{3,2,1,0:T(2,128)} copy(f32[64,8,2,2048]{0,1,2,3:T(8,128)} %convolution_bitcast_fusion) | data formatting | bytes 16777216 | tf_op jit(solution)/shard_map/cqf,sdqf->scdf/transpose | solution.py:182
  160.6 11.8 %reshape.278 = f32[64,8,4096]{2,1,0:T(8,128)} reshape(f32[64,8,2,2048]{3,2,1,0:T(2,128)} %copy.84) | data formatting | bytes 16777216 | tf_op jit(solution)/shard_map/reshape | solution.py:184
  172.5 97.8 %reduce-scatter.2.cloned.1.call-done = f32[32,8,4096]{2,1,0:T(8,128)} async-done(((f32[64,8,4096]{2,1,0:T(8,128)}), f32[32,8,4096]{2,1,0:T(8,128)}) %reduce-scatter.2.cloned.1.call-update) | async-done | bytes 4194320 | tf_op jit(solution)/shard_map/reduce_scatter | solution.py:183
  270.3 2.8 subtract_bitcast_fusion
  273.1 3.5 %fusion.20 = f32[32,32,8,128]{3,0,2,1:T(8,128)S(1)} fusion(f32[32,8,16,128]{3,1,2,0:T(8,128)S(1)} %get-tuple-element.29), kind=kOutput, calls=%fused_computation.29 | convolution fusion | flops 201333760 | bytes 6291456 | tf_op jit(solution)/shard_map/...pa,pm->...ma/dot_general | solution.py:73
  276.7 3.7 %fusion.18 = f32[32,32,8,128]{3,0,2,1:T(8,128)S(1)} fusion(f32[32,8,16,128]{3,1,2,0:T(8,128)S(1)} %get-tuple-element.29), kind=kOutput, calls=%fused_computation.27 | convolution fusion | flops 201333760 | bytes 6291456 | tf_op jit(solution)/shard_map/...pa,pm->...ma/dot_general | solution.py:76
  280.4 3.6 %convolution_subtract_fusion = f32[32,32,8,128]{3,0,2,1:T(8,128)S(1)} fusion(f32[32,32,8,128]{3,0,2,1:T(8,128)S(1)} %fusion.20, f32[32,8,16,128]{3,1,2,0:T(8,128)S(1)} %get-tuple-element.28), kind=kOutput, calls=%fused_computation.18 | convolution fusion | flops 202382336 | bytes 10485760 | tf_op jit(solution)/shard_map/...pa,pm->...ma/dot_general | solution.py:73
  283.9 4.2 %convolution_add_fusion = f32[32,32,8,128]{3,0,2,1:T(8,128)S(1)} fusion(f32[32,32,8,128]{3,0,2,1:T(8,128)S(1)} %fusion.18, f32[32,8,16,128]{3,1,2,0:T(8,128)S(1)} %get-tuple-element.28), kind=kOutput, calls=%fused_computation.17 | convolution fusion | flops 202382336 | bytes 10485760 | tf_op jit(solution)/shard_map/...pa,pm->...ma/dot_general | solution.py:76
  288.1 3.5 %fusion = f32[64,32,8,32]{0,3,2,1:T(8,128)S(1)} fusion(f32[32,32,8,128]{3,0,2,1:T(8,128)S(1)} %convolution_add_fusion, f32[32,32,8,128]{3,0,2,1:T(8,128)S(1)} %convolution_subtract_fusion, f32[32,128]{1,0:T(8,128)S(1)} %get-tuple-element.54, f32[32,128]{1,0:T(8,128)S(1)} %get-tuple-element.55), kind=kOutput, calls=%fused_computation.6 | convolution fusion | flops 808566784 | bytes 10518528 | tf_op jit(solution)/shard_map/...ma,an->...nm/dot_general | solution.py:83
  291.7 5.3 %multiply_bitcast_fusion = f32[32,8,64,32]{2,3,1,0:T(8,128)} fusion(f32[64,32,8,32]{0,3,2,1:T(8,128)S(1)} %fusion, f32[32,32,8,128]{3,0,2,1:T(8,128)S(1)} %convolution_add_fusion, f32[32,32,8,128]{3,0,2,1:T(8,128)S(1)} %convolution_subtract_fusion, f32[32,128]{1,0:T(8,128)S(1)} %get-tuple-element.54, f32[32,128]{1,0:T(8,128)S(1)} %get-tuple-element.55), kind=kOutput, calls=%fused_computation.10 | convolution fusion | flops 809615360 | bytes 12615680 | tf_op jit(solution)/shard_map/...ma,an->...nm/dot_general | solution.py:83
  296.9 7.0 %copy.89 = f32[32,8,64,32]{3,2,1,0:T(8,128)} copy(f32[32,8,64,32]{2,3,1,0:T(8,128)} %multiply_bitcast_fusion) | data formatting | bytes 4194304 | tf_op jit(solution)/shard_map/mul | solution.py:189
  303.9 7.5 %mul.267 = f32[32,8,2048]{2,1,0:T(8,128)} reshape(f32[32,8,64,32]{3,2,1,0:T(8,128)} %copy.89) | data formatting | bytes 4194304 | tf_op jit(solution)/shard_map/mul | solution.py:189
  (105 shorter events, 12.8 us)
Async XLA Ops:
  6.5 263.8 %reduce-scatter.2.cloned.1.call-start = ((), (), s32[]{:S(2)}) async-start(), calls=%async_computation.1 | async-start | bytes 12582912 | tf_op jit(solution)/shard_map/reduce_scatter | solution.py:183
  7.5 24.7 %collective-permute-start = (bf16[8,1280]{1,0:T(8,128)(2,1)S(1)}, bf16[8,1280]{1,0:T(8,128)(2,1)S(1)}, u32[]{:S(2)}, u32[]{:S(2)}) collective-permute-start(bf16[8,1280]{1,0:T(8,128)(2,1)S(1)} %get-tuple-element.44), channel_id=1, source_target_pairs={{0,2},{2,4},{4,6},{6,8},{8,10},{10,12},{12,14},{14,16},{16,18},{18... | collective-permute-start | bytes 61448 | tf_op jit(solution)/shard_map/ppermute | solution.py:144
  8.0 25.6 %collective-permute-start.1 = (bf16[8,1280]{1,0:T(8,128)(2,1)S(1)}, bf16[8,1280]{1,0:T(8,128)(2,1)S(1)}, u32[]{:S(2)}, u32[]{:S(2)}) collective-permute-start(bf16[8,1280]{1,0:T(8,128)(2,1)S(1)} %get-tuple-element.43), channel_id=1, source_target_pairs={{0,4},{2,6},{4,8},{6,10},{8,12},{10,14},{12,16},{14,18},{16,20},{1... | collective-permute-start | bytes 61448 | tf_op jit(solution)/shard_map/ppermute | solution.py:144
  10.6 23.0 %collective-permute-start.2 = (bf16[8,1280]{1,0:T(8,128)(2,1)S(1)}, bf16[8,1280]{1,0:T(8,128)(2,1)S(1)}, u32[]{:S(2)}, u32[]{:S(2)}) collective-permute-start(bf16[8,1280]{1,0:T(8,128)(2,1)S(1)} %get-tuple-element.42), channel_id=1, source_target_pairs={{0,6},{2,8},{4,10},{6,12},{8,14},{10,16},{12,18},{14,20},{16,22},{... | collective-permute-start | bytes 61448 | tf_op jit(solution)/shard_map/ppermute | solution.py:144
  13.0 21.2 %collective-permute-start.3 = (bf16[8,1280]{1,0:T(8,128)(2,1)S(1)}, bf16[8,1280]{1,0:T(8,128)(2,1)S(1)}, u32[]{:S(2)}, u32[]{:S(2)}) collective-permute-start(bf16[8,1280]{1,0:T(8,128)(2,1)S(1)} %get-tuple-element.41), channel_id=1, source_target_pairs={{0,8},{2,10},{4,12},{6,14},{8,16},{10,18},{12,20},{14,22},{16,24},... | collective-permute-start | bytes 61448 | tf_op jit(solution)/shard_map/ppermute | solution.py:144
  14.6 21.9 %collective-permute-start.4 = (bf16[8,1280]{1,0:T(8,128)(2,1)S(1)}, bf16[8,1280]{1,0:T(8,128)(2,1)S(1)}, u32[]{:S(2)}, u32[]{:S(2)}) collective-permute-start(bf16[8,1280]{1,0:T(8,128)(2,1)S(1)} %get-tuple-element.40), channel_id=1, source_target_pairs={{0,10},{2,12},{4,14},{6,16},{8,18},{10,20},{12,22},{14,24},{16,26}... | collective-permute-start | bytes 61448 | tf_op jit(solution)/shard_map/ppermute | solution.py:144
  32.2 7.5 %collective-permute-start.5 = (bf16[8,1280]{1,0:T(8,128)(2,1)S(1)}, bf16[8,1280]{1,0:T(8,128)(2,1)S(1)}, u32[]{:S(2)}, u32[]{:S(2)}) collective-permute-start(bf16[8,1280]{1,0:T(8,128)(2,1)S(1)} %get-tuple-element.39), channel_id=1, source_target_pairs={{0,12},{2,14},{4,16},{6,18},{8,20},{10,22},{12,24},{14,26},{16,28}... | collective-permute-start | bytes 61448 | tf_op jit(solution)/shard_map/ppermute | solution.py:144
  33.6 6.8 %collective-permute-start.6 = (bf16[8,1280]{1,0:T(8,128)(2,1)S(1)}, bf16[8,1280]{1,0:T(8,128)(2,1)S(1)}, u32[]{:S(2)}, u32[]{:S(2)}) collective-permute-start(bf16[8,1280]{1,0:T(8,128)(2,1)S(1)} %get-tuple-element.38), channel_id=1, source_target_pairs={{0,14},{2,16},{4,18},{6,20},{8,22},{10,24},{12,26},{14,28},{16,30}... | collective-permute-start | bytes 61448 | tf_op jit(solution)/shard_map/ppermute | solution.py:144
  33.6 8.6 %collective-permute-start.7 = (bf16[8,1280]{1,0:T(8,128)(2,1)S(1)}, bf16[8,1280]{1,0:T(8,128)(2,1)S(1)}, u32[]{:S(2)}, u32[]{:S(2)}) collective-permute-start(bf16[8,1280]{1,0:T(8,128)(2,1)S(1)} %get-tuple-element.37), channel_id=1, source_target_pairs={{0,16},{2,18},{4,20},{6,22},{8,24},{10,26},{12,28},{14,30},{16,0},... | collective-permute-start | bytes 61448 | tf_op jit(solution)/shard_map/ppermute | solution.py:144
  34.2 8.5 %collective-permute-start.8 = (bf16[8,1280]{1,0:T(8,128)(2,1)S(1)}, bf16[8,1280]{1,0:T(8,128)(2,1)S(1)}, u32[]{:S(2)}, u32[]{:S(2)}) collective-permute-start(bf16[8,1280]{1,0:T(8,128)(2,1)S(1)} %get-tuple-element.36), channel_id=1, source_target_pairs={{0,18},{2,20},{4,22},{6,24},{8,26},{10,28},{12,30},{14,0},{16,2},{... | collective-permute-start | bytes 61448 | tf_op jit(solution)/shard_map/ppermute | solution.py:144
  36.5 8.6 %collective-permute-start.9 = (bf16[8,1280]{1,0:T(8,128)(2,1)S(1)}, bf16[8,1280]{1,0:T(8,128)(2,1)S(1)}, u32[]{:S(2)}, u32[]{:S(2)}) collective-permute-start(bf16[8,1280]{1,0:T(8,128)(2,1)S(1)} %get-tuple-element.35), channel_id=1, source_target_pairs={{0,20},{2,22},{4,24},{6,26},{8,28},{10,30},{12,0},{14,2},{16,4},{1... | collective-permute-start | bytes 61448 | tf_op jit(solution)/shard_map/ppermute | solution.py:144
  39.8 6.5 %collective-permute-start.10 = (bf16[8,1280]{1,0:T(8,128)(2,1)S(1)}, bf16[8,1280]{1,0:T(8,128)(2,1)S(1)}, u32[]{:S(2)}, u32[]{:S(2)}) collective-permute-start(bf16[8,1280]{1,0:T(8,128)(2,1)S(1)} %get-tuple-element.34), channel_id=1, source_target_pairs={{0,22},{2,24},{4,26},{6,28},{8,30},{10,0},{12,2},{14,4},{16,6},{18... | collective-permute-start | bytes 61448 | tf_op jit(solution)/shard_map/ppermute | solution.py:144
  40.4 5.9 %collective-permute-start.11 = (bf16[8,1280]{1,0:T(8,128)(2,1)S(1)}, bf16[8,1280]{1,0:T(8,128)(2,1)S(1)}, u32[]{:S(2)}, u32[]{:S(2)}) collective-permute-start(bf16[8,1280]{1,0:T(8,128)(2,1)S(1)} %get-tuple-element.33), channel_id=1, source_target_pairs={{0,24},{2,26},{4,28},{6,30},{8,0},{10,2},{12,4},{14,6},{16,8},{18,... | collective-permute-start | bytes 61448 | tf_op jit(solution)/shard_map/ppermute | solution.py:144
  42.2 4.1 %collective-permute-start.12 = (bf16[8,1280]{1,0:T(8,128)(2,1)S(1)}, bf16[8,1280]{1,0:T(8,128)(2,1)S(1)}, u32[]{:S(2)}, u32[]{:S(2)}) collective-permute-start(bf16[8,1280]{1,0:T(8,128)(2,1)S(1)} %get-tuple-element.32), channel_id=1, source_target_pairs={{0,26},{2,28},{4,30},{6,0},{8,2},{10,4},{12,6},{14,8},{16,10},{18,... | collective-permute-start | bytes 61448 | tf_op jit(solution)/shard_map/ppermute | solution.py:144
  42.7 3.8 %collective-permute-start.13 = (bf16[8,1280]{1,0:T(8,128)(2,1)S(1)}, bf16[8,1280]{1,0:T(8,128)(2,1)S(1)}, u32[]{:S(2)}, u32[]{:S(2)}) collective-permute-start(bf16[8,1280]{1,0:T(8,128)(2,1)S(1)} %get-tuple-element.31), channel_id=1, source_target_pairs={{0,28},{2,30},{4,0},{6,2},{8,4},{10,6},{12,8},{14,10},{16,12},{18,... | collective-permute-start | bytes 61448 | tf_op jit(solution)/shard_map/ppermute | solution.py:144
  45.0 2.7 collective-permute-start.14
Sparse Core Ops, SparseCore 0:
  172.6 97.6 reduce-scatter.1
